TPU v7x, 32 devices: a whole 2x2x4 slice. The times are simulated.
32 devices in a mesh: atom: 8 (over z, core), energy: 4 (over y, x).
Axes of the slice: x: 2, y: 2, z: 4, core: 2. Of those that a mesh axis runs over, the one named last changes fastest.
Arguments:
- green: bfloat16 [64, 200, 512], P('atom', None, 'energy'), may hold values from -6 to 6
- coupling: bfloat16 [128, 800], P('atom'), may hold values from -0.625 to 0.625
- pairs: int32 [128, 2], P('atom'), may hold values from 0 to 63, as said below
- counts: int32 [8], P('atom'), may hold values from 8 to 16, as said below
- occupation: float32 [8], replicated, may hold values from 0.05 to 2
- offsets: int32 [8], replicated, may hold values from 1 to 64, as said below
Outputs:
- sigma: bfloat16 [64, 200, 512], P('atom', None, 'energy')
Inputs may be any that keep to these rules, and one draw needn't show every extreme that they name: `pairs`: slot s lies in partition p = s // 16; its first atom is one of partition p, atoms p * 8 to (p + 1) * 8 - 1. Its second atom is another atom of partition p, or one of the first 2 atoms of partition p + 1 (then its first atom is one of the last 2 atoms of partition p), or one of the last 2 atoms of partition p - 1 (then its first atom is one of the first 2 atoms of partition p); in every partition that has such a neighbour some live slot bonds to the farthest of those 2 atoms. `counts`: some partition has all its slots live. `offsets`: some mode has the largest offset.
All inputs are finite; a program needn't handle non-finite values.
Results may differ from a plain program's by a relative error of at most 0.012.
Values may be sent and summed in bfloat16 or wider, within the bound.
A program may use at most 192 MiB of HBM per device.

v0:
```python
import functools

import jax
import jax.numpy as jnp
import numpy as np
from jax import lax
from jax.experimental import pallas as pl
from jax.experimental.pallas import tpu as pltpu
from jax.sharding import PartitionSpec as P

NORB = 10
MODES = 8
KMAX = 64
SQ = NORB * NORB
PADROW = 16
KR = NORB * PADROW
ATOMS_DEV = 8
E_DEV = 128
SLOTS = 16
MESH = pl.DeviceIdType.MESH
F32 = jnp.float32
BF16 = jnp.bfloat16
UNROLL = 2


def expansion_tables():
    first = np.zeros((128, MODES * 128), np.float32)
    second = np.zeros((128, MODES * 128), np.float32)
    for m in range(MODES):
        for j in range(NORB):
            for k in range(NORB):
                col = m * 128 + j * NORB + k
                first[m * NORB + j, col] = 1
                second[m * NORB + k, col] = 1
    return first, second


def row_tables():
    spread = np.zeros((256, 2 * SQ), np.float32)
    collect = np.zeros((2 * SQ, 2 * KR), np.float32)
    for part in range(2):
        for r in range(SQ):
            spread[part * 128 + r, part * SQ + r] = 1
            collect[part * SQ + r, part * KR + (r // NORB) * PADROW + r % NORB] = 1
    return spread, collect


def exchange_kernel(na, ne, green, cct, meta, hl, hr, rc, rl, rr, cn, mn, to_r, to_l, rim_r, rim_l, send, recv):
    p = lax.axis_index("atom")
    q = lax.axis_index("energy")
    up, down = p < na - 1, p > 0
    right, left = q < ne - 1, q > 0
    where_to = {
        (0, 1): right,
        (0, -1): left,
        (1, 0): up,
        (-1, 0): down,
        (1, 1): up & right,
        (1, -1): up & left,
        (-1, 1): down & right,
        (-1, -1): down & left,
    }

    barrier = pltpu.get_barrier_semaphore()
    for (da, de), there in where_to.items():
        @pl.when(there)
        def _(da=da, de=de):
            pl.semaphore_signal(barrier, inc=1, device_id={"atom": p + da, "energy": q + de}, device_id_type=MESH)

    low = lax.broadcasted_iota(jnp.int32, (2 * SQ, E_DEV), 1) < 64

    def rolled(x):
        return pltpu.roll(x.astype(F32), 64, 1)

    def mix(a, b):
        return jnp.where(low, a, b).astype(BF16)

    for i in range(4):
        near = green[i].astype(F32)
        far = rolled(green[4 + i])
        to_r[i] = mix(far, near)
        to_l[i] = mix(near, far)
    six, seven = rolled(green[6]), green[7].astype(F32)
    rim_r[0] = mix(six, seven)
    rim_l[0] = mix(seven, six)
    zero, one = green[0].astype(F32), rolled(green[1])
    rim_r[1] = mix(one, zero)
    rim_l[1] = mix(zero, one)

    @pl.when(jnp.logical_not(left))
    def _():
        hl[...] = jnp.zeros_like(hl)
        rl[...] = jnp.zeros_like(rl)

    @pl.when(jnp.logical_not(right))
    def _():
        hr[...] = jnp.zeros_like(hr)
        rr[...] = jnp.zeros_like(rr)

    @pl.when(jnp.logical_not(down))
    def _():
        rc[0:2] = jnp.zeros((2,) + rc.shape[1:], BF16)
        cn[0] = jnp.zeros(cn.shape[1:], BF16)
        mn[0] = jnp.zeros(mn.shape[1:], jnp.int32)

        @pl.when(left)
        def _():
            rl[0] = jnp.zeros(rl.shape[1:], BF16)

        @pl.when(right)
        def _():
            rr[0] = jnp.zeros(rr.shape[1:], BF16)

    @pl.when(jnp.logical_not(up))
    def _():
        rc[2:4] = jnp.zeros((2,) + rc.shape[1:], BF16)
        cn[1] = jnp.zeros(cn.shape[1:], BF16)
        mn[1] = jnp.zeros(mn.shape[1:], jnp.int32)

        @pl.when(left)
        def _():
            rl[1] = jnp.zeros(rl.shape[1:], BF16)

        @pl.when(right)
        def _():
            rr[1] = jnp.zeros(rr.shape[1:], BF16)

    plan = [
        (to_r, hl, 0, 1),
        (to_l, hr, 0, -1),
        (rim_r.at[0], rl.at[0], 1, 1),
        (rim_l.at[0], rr.at[0], 1, -1),
        (rim_r.at[1], rl.at[1], -1, 1),
        (rim_l.at[1], rr.at[1], -1, -1),
        (green.at[pl.ds(6, 2)], rc.at[pl.ds(0, 2)], 1, 0),
        (green.at[pl.ds(0, 2)], rc.at[pl.ds(2, 2)], -1, 0),
        (cct, cn.at[0], 1, 0),
        (cct, cn.at[1], -1, 0),
        (meta, mn.at[0], 1, 0),
        (meta, mn.at[1], -1, 0),
    ]
    count = sum(there.astype(jnp.int32) for there in where_to.values())
    pl.semaphore_wait(barrier, count)
    copies = []
    for i, (src, dst, da, de) in enumerate(plan):
        copy = pltpu.make_async_remote_copy(
            src_ref=src,
            dst_ref=dst,
            send_sem=send.at[i],
            recv_sem=recv.at[i],
            device_id={"atom": p + da, "energy": q + de},
            device_id_type=MESH,
        )
        copies.append((copy, where_to[da, de], where_to[-da, -de]))
        pl.when(where_to[da, de])(copy.start)
    for copy, sends, gets in copies:
        pl.when(gets)(copy.wait_recv)
        pl.when(sends)(copy.wait_send)


def exchange(na, ne, green, cct, meta):
    vm = pl.BlockSpec(memory_space=pltpu.VMEM)
    slab = (2 * SQ, E_DEV)
    shape = jax.ShapeDtypeStruct
    return pl.pallas_call(
        functools.partial(exchange_kernel, na, ne),
        out_shape=[
            shape((4,) + slab, BF16),
            shape((4,) + slab, BF16),
            shape((4,) + slab, BF16),
            shape((2,) + slab, BF16),
            shape((2,) + slab, BF16),
            shape((2,) + cct.shape, BF16),
            shape((2,) + meta.shape, jnp.int32),
        ],
        in_specs=[vm] * 3,
        out_specs=[vm] * 7,
        scratch_shapes=[
            pltpu.VMEM((4,) + slab, BF16),
            pltpu.VMEM((4,) + slab, BF16),
            pltpu.VMEM((2,) + slab, BF16),
            pltpu.VMEM((2,) + slab, BF16),
            pltpu.SemaphoreType.DMA((12,)),
            pltpu.SemaphoreType.DMA((12,)),
        ],
        compiler_params=pltpu.CompilerParams(
            collective_id=0, has_side_effects=True, vmem_limit_bytes=24 * 2**20
        ),
        name="exchange",
    )(green, cct, meta)


def born_kernel(
    meta, mn, occupation, offsets, green, hl, hr, rc, rl, rr, ccc, cct, cn, first, second, spread, collect,
    out, ext, shifts, data, cc1, cc2, acc, kron, t_list, d_list, o_list,
):
    def place(rel):
        own = jnp.where(rel < 4, rel, rel + 2)
        below = jnp.where(rel == -2, 10, 4)
        above = jnp.where(rel == 8, 5, 11)
        return jnp.where(rel < 0, below, jnp.where(rel > 7, above, own))

    def append(n, keep, t, d, o):
        t_list[n] = t
        d_list[n] = d
        o_list[n] = o
        return n + keep.astype(jnp.int32)

    def listing(s, n):
        a, b = meta[0, s], meta[1, s]
        live = s < meta[2, 0]
        n = append(n, live, s, place(b), a)
        n = append(n, live & (b >= 0) & (b < 8), SLOTS + s, place(a), b)
        a, b = mn[0, 0, s] - 8, mn[0, 1, s] - 8
        n = append(n, (s < mn[0, 2, 0]) & (b >= 0) & (b < 8), 2 * SLOTS + s, place(a), b)
        a, b = mn[1, 0, s] + 8, mn[1, 1, s] + 8
        n = append(n, (s < mn[1, 2, 0]) & (b >= 0) & (b < 8), 3 * SLOTS + s, place(a), b)
        return n

    total = lax.fori_loop(0, SLOTS, listing, 0)
    for u in range(UNROLL):
        t_list[total + u] = 0
        d_list[total + u] = 0
        o_list[total + u] = ATOMS_DEV

    row = lax.broadcasted_iota(jnp.int32, (2 * E_DEV, E_DEV), 0)
    col = lax.broadcasted_iota(jnp.int32, (2 * E_DEV, E_DEV), 1)
    halo = row - E_DEV
    for kind in range(2):
        if kind == 0:
            energy = jnp.where(halo < 64, halo + 128, halo - 128)
        else:
            energy = jnp.where(halo < 64, halo - 64, halo + 64)
        delta = jnp.where(row < E_DEV, row, energy) - col
        for m in range(MODES):
            n, k = occupation[m], offsets[m]
            value = jnp.where(delta == -k, n, jnp.where(delta == k, n + 1.0, 0.0))
            shifts[kind, m // 2, :, (m % 2) * 128 : (m % 2) * 128 + 128] = value.astype(BF16)

    low = lax.broadcasted_iota(jnp.int32, (2 * SQ, E_DEV), 1) < 64

    def widen(d, centre, under, over):
        ext[d, :, 0:E_DEV] = centre
        ext[d, :, E_DEV:] = jnp.where(low, under.astype(F32), over.astype(F32)).astype(BF16)

    for i in range(4):
        widen(i, green[i], hr[i], hl[i])
        widen(6 + i, green[4 + i], hl[i], hr[i])
    widen(4, rc[1], rr[0], rl[0])
    widen(5, rc[2], rr[1], rl[1])
    widen(10, rc[0], rl[0], rr[0])
    widen(11, rc[3], rl[1], rr[1])

    def shift_atom(d, carry):
        kind = jnp.where(d < 6, 0, 1)
        rows = jnp.dot(spread[...], ext[d], preferred_element_type=F32).astype(BF16)
        for pair in range(MODES // 2):
            both = jnp.dot(rows, shifts[kind, pair], preferred_element_type=F32).astype(BF16)
            for half in range(2):
                at = (2 * pair + half) * 128
                for part in range(2):
                    data[d, at : at + 128, part * 128 : part * 128 + 128] = both[
                        part * 128 : part * 128 + 128, half * 128 : half * 128 + 128
                    ]
        return carry

    lax.fori_loop(0, ATOMS_DEV + 4, shift_atom, 0)

    for i, source in enumerate((ccc, cct, cn.at[0], cn.at[1])):
        rows = source[...].reshape(SLOTS * PADROW, 128)
        at = i * SLOTS * PADROW
        cc1[at : at + SLOTS * PADROW] = jnp.dot(rows, first[...], preferred_element_type=F32)
        cc2[at : at + SLOTS * PADROW] = jnp.dot(rows, second[...], preferred_element_type=F32)

    acc[...] = jnp.zeros_like(acc)

    def visit(step, carry):
        for u in range(UNROLL):
            at = step * UNROLL + u
            t, d, o = t_list[at], d_list[at], o_list[at]
            base = pl.multiple_of(t * PADROW, PADROW)
            right = cc2[pl.ds(base, PADROW), :]
            for i in range(NORB):
                left = cc1[pl.ds(base + i, 1), :]
                kron[u, i * PADROW : (i + 1) * PADROW, :] = (left * right).astype(BF16)
            acc[o] += jnp.dot(kron[u], data[d], preferred_element_type=F32)
        return carry

    lax.fori_loop(0, lax.div(total + UNROLL - 1, UNROLL), visit, 0)

    for o in range(ATOMS_DEV):
        mine = acc[o].astype(BF16)
        tall = jnp.concatenate([mine[:, :E_DEV], mine[:, E_DEV:]], axis=0)
        out[o] = jnp.dot(collect[...], tall, preferred_element_type=F32).astype(BF16)


def born(meta, mn, occupation, offsets, *arrays):
    vm = pl.BlockSpec(memory_space=pltpu.VMEM)
    sm = pl.BlockSpec(memory_space=pltpu.SMEM)
    rows = 4 * SLOTS * PADROW
    return pl.pallas_call(
        born_kernel,
        out_shape=jax.ShapeDtypeStruct((ATOMS_DEV, 2 * SQ, E_DEV), BF16),
        in_specs=[sm] * 4 + [vm] * len(arrays),
        out_specs=vm,
        scratch_shapes=[
            pltpu.VMEM((ATOMS_DEV + 4, 2 * SQ, 2 * E_DEV), BF16),
            pltpu.VMEM((2, MODES // 2, 2 * E_DEV, 256), BF16),
            pltpu.VMEM((ATOMS_DEV + 4, MODES * 128, 2 * E_DEV), BF16),
            pltpu.VMEM((rows, MODES * 128), F32),
            pltpu.VMEM((rows, MODES * 128), F32),
            pltpu.VMEM((ATOMS_DEV + 1, KR, 2 * E_DEV), F32),
            pltpu.VMEM((UNROLL, KR, MODES * 128), BF16),
            pltpu.SMEM((4 * SLOTS + UNROLL,), jnp.int32),
            pltpu.SMEM((4 * SLOTS + UNROLL,), jnp.int32),
            pltpu.SMEM((4 * SLOTS + UNROLL,), jnp.int32),
        ],
        compiler_params=pltpu.CompilerParams(vmem_limit_bytes=48 * 2**20),
        name="born",
    )(meta, mn, occupation, offsets, *arrays)


def per_device(na, ne, green, coupling, pairs, counts, occupation, offsets):
    base = lax.axis_index("atom") * ATOMS_DEV
    blocks = coupling.reshape(SLOTS, MODES, NORB, NORB)
    room = ((0, 0), (0, PADROW - NORB), (0, 128 - MODES * NORB))
    ccc = jnp.pad(blocks.transpose(0, 2, 1, 3).reshape(SLOTS, NORB, MODES * NORB), room)
    cct = jnp.pad(blocks.transpose(0, 3, 1, 2).reshape(SLOTS, NORB, MODES * NORB), room)
    rows = jnp.concatenate([(pairs - base).T, jnp.broadcast_to(counts, (1, SLOTS))], axis=0)
    meta = jnp.pad(rows, ((0, 5), (0, 128 - SLOTS)))
    hl, hr, rc, rl, rr, cn, mn = exchange(na, ne, green, cct, meta)
    tables = [jnp.asarray(table, BF16) for table in expansion_tables() + row_tables()]
    return born(meta, mn, occupation, offsets, green, hl, hr, rc, rl, rr, ccc, cct, cn, *tables)


def solution(mesh):
    placed = (P("atom", None, "energy"), P("atom", None), P("atom", None), P("atom"), P(), P())
    return jax.shard_map(
        functools.partial(per_device, mesh.shape["atom"], mesh.shape["energy"]),
        mesh=mesh,
        in_specs=placed,
        out_specs=P("atom", None, "energy"),
        check_vma=False,
    )
```

profile of v0, /device:TPU:10, one launch (start us, length us, event | category | flops | bytes accessed | tf_op | source)
XLA Modules:
  0.0 37.6 jit_solution(12619295797768944768)
XLA Ops:
  0.7 0.0 copy-start.7
  0.7 0.7 %copy-done.7 = s32[16,2]{0,1:T(2,128)S(1)} copy-done((s32[16,2]{0,1:T(2,128)S(1)}, s32[16,2]{0,1:T(2,128)}, u32[]{:S(2)}) %copy-start.7) | copy-done | bytes 152
  1.3 0.9 %copy.13 = bf16[16,800]{0,1:T(8,128)(2,1)S(1)} copy(bf16[16,800]{1,0:T(8,128)(2,1)} %param.11) | data formatting | bytes 51200 | tf_op args[1]
  2.3 0.1 reshape.12
  2.4 0.3 copy.15
  2.7 0.0 copy-start.3
  2.7 0.0 copy-start.4
  2.8 0.6 %copy.20 = bf16[16,10,8,10]{3,2,1,0:T(8,128)(2,1)S(1)} copy(bf16[16,10,8,10]{0,3,1,2:T(8,128)(2,1)S(1)} %bitcast.13) | data formatting | bytes 51200 | tf_op jit(solution)/shard_map/reshape | solution.py:327
  3.4 0.0 copy-start
  3.4 0.2 reshape.15
  3.6 0.0 copy-start.2
  3.6 0.7 %copy-done = bf16[8,200,128]{2,1,0:T(8,128)(2,1)S(1)} copy-done((bf16[8,200,128]{2,1,0:T(8,128)(2,1)S(1)}, bf16[8,200,128]{2,1,0:T(8,128)(2,1)}, u32[]{:S(2)}) %copy-start) | copy-done | bytes 409624
  4.4 0.0 copy-start.1
  4.4 17.9 %exchange.1 = (bf16[4,200,128]{2,1,0:T(8,128)(2,1)S(1)}, bf16[4,200,128]{2,1,0:T(8,128)(2,1)S(1)}, bf16[4,200,128]{2,1,0:T(8,128)(2,1)S(1)}, bf16[2,200,128]{2,1...) custom-call(bf16[8,200,128]{2,1,0:T(8,128)(2,1)S(1)} %copy-done, ...), custom_call_target="tpu_custom_call" | custom-call | tf_op jit(solution)/shard_map/exchange/pallas_call | solution.py:165
  22.3 0.0 copy-start.5
  22.3 0.0 copy-start.6
  22.3 0.0 copy-done.3
  22.3 0.0 copy-done.4
  22.3 0.0 copy-done.2
  22.4 0.0 copy-done.1
  22.4 0.6 %copy-done.5 = f32[8]{0:T(128)S(1)} copy-done((f32[8]{0:T(128)S(1)}, f32[8]{0:T(128)}, u32[]{:S(2)}) %copy-start.5) | copy-done | bytes 56
  23.0 0.0 copy-done.6
  23.0 14.7 %born.1 = bf16[8,200,128]{2,1,0:T(8,128)(2,1)} custom-call(s32[8,128]{1,0:T(8,128)S(1)} %select_select_fusion.meta, s32[2,8,128]{2,1,0:T(8,128)S(1)} %get-tuple-element.12.mn, f32[8]{0:T(128)S(1)} %copy-done.5, s32[8]{0:T(128)S(1)} %copy-done.6, bf16[8,200,128]{2,1,0:T(8,128)(2,1)S(1)} %copy-done, bf16[4,200,128]{2,1,0:T(8,128)(2,1)S(1)} %get-tuple-element.13.hl, ...), custom_call_target="tpu_custom_call" | custom-call | tf_op jit(solution)/shard_map/born/pallas_call | solution.py:301
  (4 shorter events, 0.1 us)
Async XLA Ops:
  0.7 0.7 %copy-start.7 = (s32[16,2]{0,1:T(2,128)S(1)}, s32[16,2]{0,1:T(2,128)}, u32[]{:S(2)}) copy-start(s32[16,2]{0,1:T(2,128)} %param.12) | copy-start | bytes 388
  2.7 19.6 %copy-start.3 = (bf16[200,320]{1,0:T(8,128)(2,1)S(1)}, bf16[200,320]{1,0:T(8,128)(2,1)}, u32[]{:S(2)}) copy-start(bf16[200,320]{1,0:T(8,128)(2,1)} %constant.23.clone.collect) | copy-start | bytes 384004
  2.7 19.6 %copy-start.4 = (bf16[256,200]{1,0:T(8,128)(2,1)S(1)}, bf16[256,200]{1,0:T(8,128)(2,1)}, u32[]{:S(2)}) copy-start(bf16[256,200]{1,0:T(8,128)(2,1)} %constant.22.clone.spread) | copy-start | bytes 307204
  3.4 1.0 %copy-start = (bf16[8,200,128]{2,1,0:T(8,128)(2,1)S(1)}, bf16[8,200,128]{2,1,0:T(8,128)(2,1)}, u32[]{:S(2)}) copy-start(bf16[8,200,128]{2,1,0:T(8,128)(2,1)} %green.3) | copy-start | bytes 1228804
  3.6 18.7 %copy-start.2 = (bf16[128,1024]{1,0:T(8,128)(2,1)S(1)}, bf16[128,1024]{1,0:T(8,128)(2,1)}, u32[]{:S(2)}) copy-start(bf16[128,1024]{1,0:T(8,128)(2,1)} %constant.20.clone.first) | copy-start | bytes 786436
  4.4 18.0 %copy-start.1 = (bf16[128,1024]{1,0:T(8,128)(2,1)S(1)}, bf16[128,1024]{1,0:T(8,128)(2,1)}, u32[]{:S(2)}) copy-start(bf16[128,1024]{1,0:T(8,128)(2,1)} %constant.21.clone.second) | copy-start | bytes 786436
  22.3 0.7 %copy-start.5 = (f32[8]{0:T(128)S(1)}, f32[8]{0:T(128)}, u32[]{:S(2)}) copy-start(f32[8]{0:T(128)} %occupation.1) | copy-start | bytes 100
  22.3 0.7 %copy-start.6 = (s32[8]{0:T(128)S(1)}, s32[8]{0:T(128)}, u32[]{:S(2)}) copy-start(s32[8]{0:T(128)} %offsets.1) | copy-start | bytes 100
where the time goes:
time: 37.7 us; the launch traced here: 37.6 us
  Pallas kernels  32.6 us (86%)
  local copies, waits for them, and re-layouts  4.25 us (11%)
  between operations  0.8 us (2%)
    pallas_call x1, Pallas kernels, exchange(): pl.pallas_call(functools.partial(exchange_kernel, na, ne), out_shape=[sha...  17.9 us
    pallas_call x1, Pallas kernels, born(): pl.pallas_call(born_kernel, out_shape=jax.ShapeDtypeStruct((ATOMS_DEV, 2...  14.7 us
    unnamed x17, local copies, waits for them, and re-layouts  2.96 us
    reshape x2, local copies, waits for them, and re-layouts, per_device(): blocks.transpose(0, 2, 1, 3).reshape(SLOTS, NORB, MODES * NORB)  0.82 us

commit v1 on v0

v1 whole, which is shorter than its diff:
```python
import functools

import jax
import jax.numpy as jnp
import numpy as np
from jax import lax
from jax.experimental import pallas as pl
from jax.experimental.pallas import tpu as pltpu
from jax.sharding import PartitionSpec as P

NORB = 10
MODES = 8
KMAX = 64
SQ = NORB * NORB
PADROW = 16
KR = NORB * PADROW
ATOMS_DEV = 8
E_DEV = 128
SLOTS = 16
MESH = pl.DeviceIdType.MESH
F32 = jnp.float32
BF16 = jnp.bfloat16
UNROLL = 2


def expansion_tables():
    tables = np.zeros((4, SQ, NORB * 128), np.float32)
    for i in range(NORB):
        for j in range(NORB):
            for k in range(NORB):
                col = i * 128 + j * NORB + k
                tables[0, i * NORB + j, col] = 1
                tables[1, i * NORB + k, col] = 1
                tables[2, j * NORB + i, col] = 1
                tables[3, k * NORB + i, col] = 1
    return tables


def row_tables():
    spread = np.zeros((256, 2 * SQ), np.float32)
    collect = np.zeros((2 * SQ, 2 * KR), np.float32)
    for part in range(2):
        for r in range(SQ):
            spread[part * 128 + r, part * SQ + r] = 1
            collect[part * SQ + r, part * KR + (r // NORB) * PADROW + r % NORB] = 1
    return spread, collect


def exchange_kernel(
    na, ne, occupation, offsets, green, coupling, meta, tables, spread,
    data, left_cc, right_cc, mn,
    hl, hr, rc, rh, coup_n, to_r, to_l, forward, shifts, send, recv,
):
    p = lax.axis_index("atom")
    q = lax.axis_index("energy")
    up, down = p < na - 1, p > 0
    right, left = q < ne - 1, q > 0
    where_to = {(0, 1): right, (0, -1): left, (1, 0): up, (-1, 0): down}

    def peer(da, de):
        return {"atom": p + da, "energy": q + de}

    barrier = pltpu.get_barrier_semaphore()
    for (da, de), there in where_to.items():
        @pl.when(there)
        def _(da=da, de=de):
            pl.semaphore_signal(barrier, inc=1, device_id=peer(da, de), device_id_type=MESH)

    low = lax.broadcasted_iota(jnp.int32, (2 * SQ, E_DEV), 1) < 64

    def mix(a, b):
        return jnp.where(low, a, b).astype(BF16)

    def far_atom(c):
        return c + 6 if c < 2 else c + 2

    for c in range(4):
        near = green[c].astype(F32)
        far = pltpu.roll(green[far_atom(c)].astype(F32), 64, 1)
        to_r[c] = mix(far, near)
        to_l[c] = mix(near, far)

    def clear(ref):
        ref[...] = jnp.zeros(ref.shape, ref.dtype)

    @pl.when(jnp.logical_not(left))
    def _():
        clear(hl)

    @pl.when(jnp.logical_not(right))
    def _():
        clear(hr)

    for side, there in ((0, down), (1, up)):
        @pl.when(jnp.logical_not(there))
        def _(side=side):
            clear(rc.at[pl.ds(2 * side, 2)])
            clear(rh.at[pl.ds(2 * side, 2)])
            clear(coup_n.at[side])
            clear(mn.at[side])

    slots = iter(range(16))

    def copy_to(source, target, da, de):
        i = next(slots)
        copy = pltpu.make_async_remote_copy(
            src_ref=source,
            dst_ref=target,
            send_sem=send.at[i],
            recv_sem=recv.at[i],
            device_id=peer(da, de),
            device_id_type=MESH,
        )
        return copy, where_to[da, de], where_to[-da, -de]

    def start(items):
        for copy, sends, _ in items:
            pl.when(sends)(copy.start)

    def arrive(items):
        for copy, _, gets in items:
            pl.when(gets)(copy.wait_recv)

    def sent(items):
        for copy, sends, _ in items:
            pl.when(sends)(copy.wait_send)

    halos = [
        [copy_to(to_r.at[c], hl.at[c], 0, 1), copy_to(to_l.at[c], hr.at[c], 0, -1)] for c in range(4)
    ]
    small = [
        copy_to(coupling, coup_n.at[0], 1, 0),
        copy_to(coupling, coup_n.at[1], -1, 0),
        copy_to(meta, mn.at[0], 1, 0),
        copy_to(meta, mn.at[1], -1, 0),
    ]
    rims = [
        copy_to(green.at[pl.ds(6, 2)], rc.at[pl.ds(0, 2)], 1, 0),
        copy_to(green.at[pl.ds(0, 2)], rc.at[pl.ds(2, 2)], -1, 0),
    ]
    passed = [
        copy_to(forward.at[pl.ds(0, 2)], rh.at[pl.ds(0, 2)], 1, 0),
        copy_to(forward.at[pl.ds(2, 2)], rh.at[pl.ds(2, 2)], -1, 0),
    ]

    pl.semaphore_wait(barrier, sum(there.astype(jnp.int32) for there in where_to.values()))
    start(halos[0])
    start(halos[1])
    start(small)
    start(rims)
    start(halos[2])
    start(halos[3])

    row = lax.broadcasted_iota(jnp.int32, (2 * E_DEV, E_DEV), 0)
    col = lax.broadcasted_iota(jnp.int32, (2 * E_DEV, E_DEV), 1)
    outer = row - E_DEV
    for kind in range(2):
        if kind == 0:
            energy = jnp.where(outer < 64, outer + 128, outer - 128)
        else:
            energy = jnp.where(outer < 64, outer - 64, outer + 64)
        delta = jnp.where(row < E_DEV, row, energy) - col
        for m in range(MODES):
            n, k = occupation[m], offsets[m]
            value = jnp.where(delta == -k, n, jnp.where(delta == k, n + 1.0, 0.0))
            shifts[kind, m // 2, :, (m % 2) * 128 : (m % 2) * 128 + 128] = value.astype(BF16)

    def expand(source, table, target):
        rows = jnp.concatenate([source[:, m * SQ : (m + 1) * SQ] for m in range(MODES)], axis=0)
        wide = jnp.dot(rows, tables[table], preferred_element_type=F32)
        for m in range(MODES):
            for i in range(NORB):
                target[m, i * SLOTS : (i + 1) * SLOTS, :] = wide[
                    m * SLOTS : (m + 1) * SLOTS, i * 128 : (i + 1) * 128
                ]

    for group in range(4):
        right_cc[group, :, NORB * SLOTS :, :] = jnp.zeros((MODES, 256 - NORB * SLOTS, 128), F32)
    expand(coupling, 0, left_cc.at[0])
    expand(coupling, 1, right_cc.at[0])
    expand(coupling, 2, left_cc.at[1])
    expand(coupling, 3, right_cc.at[1])
    arrive(small)
    for side in range(2):
        expand(coup_n.at[side], 2, left_cc.at[2 + side])
        expand(coup_n.at[side], 3, right_cc.at[2 + side])

    def shift(d, kind, centre, halo):
        wide = jnp.concatenate([centre, halo], axis=1)
        rows = jnp.dot(spread[...], wide, preferred_element_type=F32).astype(BF16)
        for pair in range(MODES // 2):
            both = jnp.dot(rows, shifts[kind, pair], preferred_element_type=F32).astype(BF16)
            for half in range(2):
                at = (2 * pair + half) * 128
                for part in range(2):
                    data[d, at : at + 128, part * 128 : part * 128 + 128] = both[
                        part * 128 : part * 128 + 128, half * 128 : half * 128 + 128
                    ]

    def own_halos(c):
        lower, upper = hl[c].astype(F32), hr[c].astype(F32)
        return mix(upper, lower), mix(lower, upper)

    def shift_own(c, far):
        near_halo, far_halo = own_halos(c)
        shift(c, 0, green[c], near_halo)
        shift(6 + c, 1, green[far], far_halo)

    arrive(halos[0])
    arrive(halos[1])
    for c in range(2):
        near_halo, far_halo = own_halos(c)
        forward[c] = far_halo
        forward[2 + c] = near_halo
    start(passed)

    def first_half(c, carry):
        shift_own(c, c + 6)
        return carry

    lax.fori_loop(0, 2, first_half, 0)
    arrive(halos[2])
    shift_own(2, 4)
    arrive(rims)
    arrive(passed)

    def rim(c, carry):
        shift(4 + c, 0, rc[2 + c], rh[2 + c])
        shift(10 + c, 1, rc[c], rh[c])
        return carry

    lax.fori_loop(0, 2, rim, 0)
    arrive(halos[3])
    shift_own(3, 5)
    for items in halos + [small, rims, passed]:
        sent(items)


def exchange(na, ne, occupation, offsets, green, coupling, meta, tables, spread):
    vm = pl.BlockSpec(memory_space=pltpu.VMEM)
    sm = pl.BlockSpec(memory_space=pltpu.SMEM)
    slab = (2 * SQ, E_DEV)
    shape = jax.ShapeDtypeStruct
    return pl.pallas_call(
        functools.partial(exchange_kernel, na, ne),
        out_shape=[
            shape((ATOMS_DEV + 4, MODES * 128, 2 * E_DEV), BF16),
            shape((4, MODES, 256, 128), F32),
            shape((4, MODES, 256, 128), F32),
            shape((2,) + meta.shape, jnp.int32),
        ],
        in_specs=[sm] * 2 + [vm] * 5,
        out_specs=[vm] * 4,
        scratch_shapes=[
            pltpu.VMEM((4,) + slab, BF16),
            pltpu.VMEM((4,) + slab, BF16),
            pltpu.VMEM((4,) + slab, BF16),
            pltpu.VMEM((4,) + slab, BF16),
            pltpu.VMEM((2,) + coupling.shape, BF16),
            pltpu.VMEM((4,) + slab, BF16),
            pltpu.VMEM((4,) + slab, BF16),
            pltpu.VMEM((4,) + slab, BF16),
            pltpu.VMEM((2, MODES // 2, 2 * E_DEV, 256), BF16),
            pltpu.SemaphoreType.DMA((16,)),
            pltpu.SemaphoreType.DMA((16,)),
        ],
        compiler_params=pltpu.CompilerParams(
            collective_id=0, has_side_effects=True, vmem_limit_bytes=32 * 2**20
        ),
        name="exchange",
    )(occupation, offsets, green, coupling, meta, tables, spread)


def born_kernel(meta, mn, data, left_cc, right_cc, collect, out, acc, kron, t_list, d_list, o_list):
    base = lax.axis_index("atom") * ATOMS_DEV

    def place(rel):
        own = jnp.where((rel == 4) | (rel == 5), rel + 4, rel)
        return jnp.where(rel < 0, rel + 12, jnp.where(rel > 7, rel - 4, own))

    def append(n, keep, t, d, o):
        t_list[n] = t
        d_list[n] = d
        o_list[n] = o
        return n + keep.astype(jnp.int32)

    def listing(s, n):
        a, b = meta[0, s] - base, meta[1, s] - base
        live = s < meta[2, 0]
        n = append(n, live, s, place(b), a)
        n = append(n, live & (b >= 0) & (b < 8), SLOTS + s, place(a), b)
        for side in range(2):
            a, b = mn[side, 0, s] - base, mn[side, 1, s] - base
            live = (s < mn[side, 2, 0]) & (b >= 0) & (b < 8)
            n = append(n, live, (2 + side) * SLOTS + s, place(a), b)
        return n

    total = lax.fori_loop(0, SLOTS, listing, 0)
    for u in range(UNROLL):
        t_list[total + u] = 0
        d_list[total + u] = 0
        o_list[total + u] = ATOMS_DEV

    acc[...] = jnp.zeros_like(acc)

    def visit(step, carry):
        for u in range(UNROLL):
            at = step * UNROLL + u
            t, d, o = t_list[at], d_list[at], o_list[at]
            group, s = lax.shift_right_logical(t, 4), t & 15
            for m in range(MODES):
                right = right_cc[group, m, pl.ds(s, PADROW, stride=SLOTS), :]
                for i in range(NORB):
                    left = left_cc[group, m, pl.ds(i * SLOTS + s, 1), :]
                    kron[u, i * PADROW : (i + 1) * PADROW, m * 128 : (m + 1) * 128] = (left * right).astype(BF16)
            acc[o] += jnp.dot(kron[u], data[d], preferred_element_type=F32)
        return carry

    lax.fori_loop(0, lax.div(total + UNROLL - 1, UNROLL), visit, 0)

    for o in range(ATOMS_DEV):
        mine = acc[o].astype(BF16)
        tall = jnp.concatenate([mine[:, :E_DEV], mine[:, E_DEV:]], axis=0)
        out[o] = jnp.dot(collect[...], tall, preferred_element_type=F32).astype(BF16)


def born(meta, mn, *arrays):
    vm = pl.BlockSpec(memory_space=pltpu.VMEM)
    sm = pl.BlockSpec(memory_space=pltpu.SMEM)
    return pl.pallas_call(
        born_kernel,
        out_shape=jax.ShapeDtypeStruct((ATOMS_DEV, 2 * SQ, E_DEV), BF16),
        in_specs=[sm] * 2 + [vm] * len(arrays),
        out_specs=vm,
        scratch_shapes=[
            pltpu.VMEM((ATOMS_DEV + 1, KR, 2 * E_DEV), F32),
            pltpu.VMEM((UNROLL, KR, MODES * 128), BF16),
            pltpu.SMEM((4 * SLOTS + UNROLL,), jnp.int32),
            pltpu.SMEM((4 * SLOTS + UNROLL,), jnp.int32),
            pltpu.SMEM((4 * SLOTS + UNROLL,), jnp.int32),
        ],
        compiler_params=pltpu.CompilerParams(vmem_limit_bytes=32 * 2**20),
        name="born",
    )(meta, mn, *arrays)


def per_device(na, ne, green, coupling, pairs, counts, occupation, offsets):
    meta = jnp.concatenate([pairs.T, jnp.broadcast_to(counts, (1, SLOTS))], axis=0)
    spread, collect = row_tables()
    tables = jnp.asarray(expansion_tables(), BF16)
    data, left_cc, right_cc, mn = exchange(
        na, ne, occupation, offsets, green, coupling, meta, tables, jnp.asarray(spread, BF16)
    )
    return born(meta, mn, data, left_cc, right_cc, jnp.asarray(collect, BF16))


def solution(mesh):
    placed = (P("atom", None, "energy"), P("atom", None), P("atom", None), P("atom"), P(), P())
    return jax.shard_map(
        functools.partial(per_device, mesh.shape["atom"], mesh.shape["energy"]),
        mesh=mesh,
        in_specs=placed,
        out_specs=P("atom", None, "energy"),
        check_vma=False,
    )
```

time: 37.7 us -> 34.2 us (0.907)
  the two profiles are of different devices: /device:TPU:10 before, /device:TPU:1 now
where the time goes in v1:
time: 34.2 us; the launch traced here: 34.5 us
  Pallas kernels  27 us (79%)
  local copies, waits for them, and re-layouts  6.78 us (20%)
  between operations  0.68 us (2%)
    pallas_call x1, Pallas kernels, exchange(): pl.pallas_call(functools.partial(exchange_kernel, na, ne), out_shape=[sha...  17 us
    pallas_call x1, Pallas kernels, born(): pl.pallas_call(born_kernel, out_shape=jax.ShapeDtypeStruct((ATOMS_DEV, 2...  10.1 us
    unnamed x14, local copies, waits for them, and re-layouts  6.1 us
    concatenate x1, local copies, waits for them, and re-layouts, per_device(): jnp.concatenate([pairs.T, jnp.broadcast_to(counts, (1, SLOTS))], axis=0)  0.69 us

profile of v1, /device:TPU:1, one launch (start us, length us, event | category | flops | bytes accessed | tf_op | source)
XLA Modules:
  0.0 34.5 jit_solution(751918547770050649)
XLA Ops:
  0.7 0.7 %concatenate.3.meta = s32[3,16]{1,0:T(4,128)S(1)} pad(s32[2,16]{1,0:T(2,128)} %bitcast.3, s32[]{:T(128)} %bitcast.2), padding=0_1x0_0 | pad | bytes 324 | tf_op jit(solution)/shard_map/concatenate | solution.py:348
  1.3 0.0 copy-start
  1.3 1.2 %copy-done = bf16[4,100,1280]{2,1,0:T(8,128)(2,1)S(1)} copy-done((bf16[4,100,1280]{2,1,0:T(8,128)(2,1)S(1)}, bf16[4,100,1280]{2,1,0:T(8,128)(2,1)}, u32[]{:S(2)}) %copy-start) | copy-done | bytes 1024024
  2.6 0.0 copy-start.1
  2.6 1.0 %copy-done.1 = bf16[8,200,128]{2,1,0:T(8,128)(2,1)S(1)} copy-done((bf16[8,200,128]{2,1,0:T(8,128)(2,1)S(1)}, bf16[8,200,128]{2,1,0:T(8,128)(2,1)}, u32[]{:S(2)}) %copy-start.1) | copy-done | bytes 409624
  3.6 0.0 copy-start.3
  3.6 0.9 %copy-done.3 = bf16[256,200]{1,0:T(8,128)(2,1)S(1)} copy-done((bf16[256,200]{1,0:T(8,128)(2,1)S(1)}, bf16[256,200]{1,0:T(8,128)(2,1)}, u32[]{:S(2)}) %copy-start.3) | copy-done | bytes 102424
  4.5 0.0 copy-start.4
  4.5 0.7 %copy-done.4 = bf16[16,800]{1,0:T(8,128)(2,1)S(1)} copy-done((bf16[16,800]{1,0:T(8,128)(2,1)S(1)}, bf16[16,800]{1,0:T(8,128)(2,1)}, u32[]{:S(2)}) %copy-start.4) | copy-done | bytes 25624
  5.2 0.0 copy-start.5
  5.2 0.7 %copy-done.5 = f32[8]{0:T(128)S(1)} copy-done((f32[8]{0:T(128)S(1)}, f32[8]{0:T(128)}, u32[]{:S(2)}) %copy-start.5) | copy-done | bytes 56
  5.9 0.0 copy-start.6
  5.9 0.7 %copy-done.6 = s32[8]{0:T(128)S(1)} copy-done((s32[8]{0:T(128)S(1)}, s32[8]{0:T(128)}, u32[]{:S(2)}) %copy-start.6) | copy-done | bytes 56
  6.5 17.0 %exchange.1 = (bf16[12,1024,256]{2,1,0:T(8,128)(2,1)S(1)}, f32[4,8,256,128]{3,2,1,0:T(8,128)S(1)}, f32[4,8,256,128]{3,2,1,0:T(8,128)S(1)}, s32[2,3,16]{2,1,0:T(4,128)S(1)}) custom-call(f32[8]{0:T(128)S(1)} %copy-done.5, s32[8]{0:T(128)S(1)} %copy-done.6, bf16[8,200,128]{2,1,0:T(8,128)(2,1)S(1)} %copy-done.1, bf16[16,800]{1,0:T(8,128)(2,1)S(1)} %copy-done.4, ...), custom_call_target="tpu_custom_call" | custom-call | tf_op jit(solution)/shard_map/exchange/pallas_call | solution.py:244
  23.5 0.0 copy-start.2
  23.5 0.9 %copy-done.2 = bf16[200,320]{1,0:T(8,128)(2,1)S(1)} copy-done((bf16[200,320]{1,0:T(8,128)(2,1)S(1)}, bf16[200,320]{1,0:T(8,128)(2,1)}, u32[]{:S(2)}) %copy-start.2) | copy-done | bytes 128024
  24.4 10.1 %born.1 = bf16[8,200,128]{2,1,0:T(8,128)(2,1)} custom-call(s32[3,16]{1,0:T(4,128)S(1)} %concatenate.3.meta, s32[2,3,16]{2,1,0:T(4,128)S(1)} %get-tuple-element.9.mn, bf16[12,1024,256]{2,1,0:T(8,128)(2,1)S(1)} %get-tuple-element.10.data, f32[4,8,256,128]{3,2,1,0:T(8,128)S(1)} %get-tuple-element.11.left_cc, f32[4,8,256,128]{3,2,1,0:T(8,128)S(1)} %get-tuple-element.12.right_cc, ...), custom_call_target="tpu_custom_call" | custom-call | tf_op jit(solution)/shard_map/born/pallas_call | solution.py:330
Async XLA Ops:
  1.3 1.2 %copy-start = (bf16[4,100,1280]{2,1,0:T(8,128)(2,1)S(1)}, bf16[4,100,1280]{2,1,0:T(8,128)(2,1)}, u32[]{:S(2)}) copy-start(bf16[4,100,1280]{2,1,0:T(8,128)(2,1)} %constant.6.clone.tables) | copy-start | bytes 3072004
  2.6 1.0 %copy-start.1 = (bf16[8,200,128]{2,1,0:T(8,128)(2,1)S(1)}, bf16[8,200,128]{2,1,0:T(8,128)(2,1)}, u32[]{:S(2)}) copy-start(bf16[8,200,128]{2,1,0:T(8,128)(2,1)} %green.1) | copy-start | bytes 1228804
  3.6 0.9 %copy-start.3 = (bf16[256,200]{1,0:T(8,128)(2,1)S(1)}, bf16[256,200]{1,0:T(8,128)(2,1)}, u32[]{:S(2)}) copy-start(bf16[256,200]{1,0:T(8,128)(2,1)} %constant.7.clone.spread) | copy-start | bytes 307204
  4.5 0.7 %copy-start.4 = (bf16[16,800]{1,0:T(8,128)(2,1)S(1)}, bf16[16,800]{1,0:T(8,128)(2,1)}, u32[]{:S(2)}) copy-start(bf16[16,800]{1,0:T(8,128)(2,1)} %coupling.1) | copy-start | bytes 76804
  5.2 0.7 %copy-start.5 = (f32[8]{0:T(128)S(1)}, f32[8]{0:T(128)}, u32[]{:S(2)}) copy-start(f32[8]{0:T(128)} %occupation.1) | copy-start | bytes 100
  5.9 0.7 %copy-start.6 = (s32[8]{0:T(128)S(1)}, s32[8]{0:T(128)}, u32[]{:S(2)}) copy-start(s32[8]{0:T(128)} %offsets.1) | copy-start | bytes 100
  23.5 0.9 %copy-start.2 = (bf16[200,320]{1,0:T(8,128)(2,1)S(1)}, bf16[200,320]{1,0:T(8,128)(2,1)}, u32[]{:S(2)}) copy-start(bf16[200,320]{1,0:T(8,128)(2,1)} %constant.8.clone.collect) | copy-start | bytes 384004

commit v2 on v1

--- a/solution.py
+++ b/solution.py
@@ -2,7 +2,6 @@
 
 import jax
 import jax.numpy as jnp
-import numpy as np
 from jax import lax
 from jax.experimental import pallas as pl
 from jax.experimental.pallas import tpu as pltpu
@@ -23,33 +22,42 @@
 UNROLL = 2
 
 
-def expansion_tables():
-    tables = np.zeros((4, SQ, NORB * 128), np.float32)
+def fill_tables(tables):
+    row = lax.broadcasted_iota(jnp.int32, (SQ, 128), 0)
+    lane = lax.broadcasted_iota(jnp.int32, (SQ, 128), 1)
+    j = lax.shift_right_logical(lane * 205, 11)
+    k = lane - j * NORB
+    inside = lane < SQ
     for i in range(NORB):
-        for j in range(NORB):
-            for k in range(NORB):
-                col = i * 128 + j * NORB + k
-                tables[0, i * NORB + j, col] = 1
-                tables[1, i * NORB + k, col] = 1
-                tables[2, j * NORB + i, col] = 1
-                tables[3, k * NORB + i, col] = 1
-    return tables
-
-
-def row_tables():
-    spread = np.zeros((256, 2 * SQ), np.float32)
-    collect = np.zeros((2 * SQ, 2 * KR), np.float32)
-    for part in range(2):
-        for r in range(SQ):
-            spread[part * 128 + r, part * SQ + r] = 1
-            collect[part * SQ + r, part * KR + (r // NORB) * PADROW + r % NORB] = 1
-    return spread, collect
+        for table, want in enumerate((i * NORB + j, i * NORB + k, j * NORB + i, k * NORB + i)):
+            tables[table, :, i * 128 : (i + 1) * 128] = one_where(inside & (row == want))
+
+
+def one_where(mask):
+    return jnp.where(mask, 1.0, 0.0).astype(BF16)
+
+
+def spread_matrix():
+    row = lax.broadcasted_iota(jnp.int32, (256, 2 * SQ), 0)
+    col = lax.broadcasted_iota(jnp.int32, (256, 2 * SQ), 1)
+    first = (row < SQ) & (col == row)
+    second = (row >= 128) & (row < 128 + SQ) & (col == row - 128 + SQ)
+    return one_where(first | second)
+
+
+def collect_matrix():
+    row = lax.broadcasted_iota(jnp.int32, (2 * SQ, 2 * KR), 0)
+    col = lax.broadcasted_iota(jnp.int32, (2 * SQ, 2 * KR), 1)
+    part = jnp.where(col < KR, 0, 1)
+    at = col - part * KR
+    i, l = lax.shift_right_logical(at, 4), at & (PADROW - 1)
+    return one_where((l < NORB) & (row == part * SQ + i * NORB + l))
 
 
 def exchange_kernel(
-    na, ne, occupation, offsets, green, coupling, meta, tables, spread,
-    data, left_cc, right_cc, mn,
-    hl, hr, rc, rh, coup_n, to_r, to_l, forward, shifts, send, recv,
+    na, ne, green, pack,
+    data, left_cc, right_cc, pack_n,
+    hl, hr, rc, rh, to_r, to_l, forward, shifts, tables, spread, send, recv,
 ):
     p = lax.axis_index("atom")
     q = lax.axis_index("energy")
@@ -96,8 +104,7 @@
         def _(side=side):
             clear(rc.at[pl.ds(2 * side, 2)])
             clear(rh.at[pl.ds(2 * side, 2)])
-            clear(coup_n.at[side])
-            clear(mn.at[side])
+            clear(pack_n.at[side])
 
     slots = iter(range(16))
 
@@ -129,10 +136,8 @@
         [copy_to(to_r.at[c], hl.at[c], 0, 1), copy_to(to_l.at[c], hr.at[c], 0, -1)] for c in range(4)
     ]
     small = [
-        copy_to(coupling, coup_n.at[0], 1, 0),
-        copy_to(coupling, coup_n.at[1], -1, 0),
-        copy_to(meta, mn.at[0], 1, 0),
-        copy_to(meta, mn.at[1], -1, 0),
+        copy_to(pack, pack_n.at[0], 1, 0),
+        copy_to(pack, pack_n.at[1], -1, 0),
     ]
     rims = [
         copy_to(green.at[pl.ds(6, 2)], rc.at[pl.ds(0, 2)], 1, 0),
@@ -159,14 +164,16 @@
             energy = jnp.where(outer < 64, outer + 128, outer - 128)
         else:
             energy = jnp.where(outer < 64, outer - 64, outer + 64)
-        delta = jnp.where(row < E_DEV, row, energy) - col
+        delta = (jnp.where(row < E_DEV, row, energy) - col).astype(F32)
         for m in range(MODES):
-            n, k = occupation[m], offsets[m]
+            n, k = pack[SLOTS + 3 : SLOTS + 4, m : m + 1], pack[SLOTS + 4 : SLOTS + 5, m : m + 1]
             value = jnp.where(delta == -k, n, jnp.where(delta == k, n + 1.0, 0.0))
             shifts[kind, m // 2, :, (m % 2) * 128 : (m % 2) * 128 + 128] = value.astype(BF16)
 
     def expand(source, table, target):
-        rows = jnp.concatenate([source[:, m * SQ : (m + 1) * SQ] for m in range(MODES)], axis=0)
+        rows = jnp.concatenate(
+            [source[0:SLOTS, m * SQ : (m + 1) * SQ] for m in range(MODES)], axis=0
+        ).astype(BF16)
         wide = jnp.dot(rows, tables[table], preferred_element_type=F32)
         for m in range(MODES):
             for i in range(NORB):
@@ -176,14 +183,16 @@
 
     for group in range(4):
         right_cc[group, :, NORB * SLOTS :, :] = jnp.zeros((MODES, 256 - NORB * SLOTS, 128), F32)
-    expand(coupling, 0, left_cc.at[0])
-    expand(coupling, 1, right_cc.at[0])
-    expand(coupling, 2, left_cc.at[1])
-    expand(coupling, 3, right_cc.at[1])
+    fill_tables(tables)
+    spread[...] = spread_matrix()
+    expand(pack, 0, left_cc.at[0])
+    expand(pack, 1, right_cc.at[0])
+    expand(pack, 2, left_cc.at[1])
+    expand(pack, 3, right_cc.at[1])
     arrive(small)
     for side in range(2):
-        expand(coup_n.at[side], 2, left_cc.at[2 + side])
-        expand(coup_n.at[side], 3, right_cc.at[2 + side])
+        expand(pack_n.at[side], 2, left_cc.at[2 + side])
+        expand(pack_n.at[side], 3, right_cc.at[2 + side])
 
     def shift(d, kind, centre, halo):
         wide = jnp.concatenate([centre, halo], axis=1)
@@ -236,9 +245,8 @@
         sent(items)
 
 
-def exchange(na, ne, occupation, offsets, green, coupling, meta, tables, spread):
+def exchange(na, ne, green, pack):
     vm = pl.BlockSpec(memory_space=pltpu.VMEM)
-    sm = pl.BlockSpec(memory_space=pltpu.SMEM)
     slab = (2 * SQ, E_DEV)
     shape = jax.ShapeDtypeStruct
     return pl.pallas_call(
@@ -247,20 +255,21 @@
             shape((ATOMS_DEV + 4, MODES * 128, 2 * E_DEV), BF16),
             shape((4, MODES, 256, 128), F32),
             shape((4, MODES, 256, 128), F32),
-            shape((2,) + meta.shape, jnp.int32),
+            shape((2,) + pack.shape, F32),
         ],
-        in_specs=[sm] * 2 + [vm] * 5,
+        in_specs=[vm] * 2,
         out_specs=[vm] * 4,
         scratch_shapes=[
             pltpu.VMEM((4,) + slab, BF16),
             pltpu.VMEM((4,) + slab, BF16),
             pltpu.VMEM((4,) + slab, BF16),
             pltpu.VMEM((4,) + slab, BF16),
-            pltpu.VMEM((2,) + coupling.shape, BF16),
             pltpu.VMEM((4,) + slab, BF16),
             pltpu.VMEM((4,) + slab, BF16),
             pltpu.VMEM((4,) + slab, BF16),
             pltpu.VMEM((2, MODES // 2, 2 * E_DEV, 256), BF16),
+            pltpu.VMEM((4, SQ, NORB * 128), BF16),
+            pltpu.VMEM((256, 2 * SQ), BF16),
             pltpu.SemaphoreType.DMA((16,)),
             pltpu.SemaphoreType.DMA((16,)),
         ],
@@ -268,10 +277,26 @@
             collective_id=0, has_side_effects=True, vmem_limit_bytes=32 * 2**20
         ),
         name="exchange",
-    )(occupation, offsets, green, coupling, meta, tables, spread)
-
-
-def born_kernel(meta, mn, data, left_cc, right_cc, collect, out, acc, kron, t_list, d_list, o_list):
+    )(green, pack)
+
+
+def born_kernel(
+    pack, pack_n, data, left_cc, right_cc, out, acc, kron, collect, lists, t_list, d_list, o_list, fetch
+):
+    fetches = [
+        pltpu.make_async_copy(source.at[pl.ds(SLOTS, 8), pl.ds(0, 128)], lists.at[i], fetch.at[i])
+        for i, source in enumerate((pack, pack_n.at[0], pack_n.at[1]))
+    ]
+    for one in fetches:
+        one.start()
+    collect[...] = collect_matrix()
+    acc[...] = jnp.zeros_like(acc)
+    for one in fetches:
+        one.wait()
+
+    def entry(source, r, s):
+        return lists[source, r, s].astype(jnp.int32)
+
     base = lax.axis_index("atom") * ATOMS_DEV
 
     def place(rel):
@@ -285,37 +310,41 @@
         return n + keep.astype(jnp.int32)
 
     def listing(s, n):
-        a, b = meta[0, s] - base, meta[1, s] - base
-        live = s < meta[2, 0]
+        a, b = entry(0, 0, s) - base, entry(0, 1, s) - base
+        live = s < entry(0, 2, 0)
         n = append(n, live, s, place(b), a)
         n = append(n, live & (b >= 0) & (b < 8), SLOTS + s, place(a), b)
         for side in range(2):
-            a, b = mn[side, 0, s] - base, mn[side, 1, s] - base
-            live = (s < mn[side, 2, 0]) & (b >= 0) & (b < 8)
+            a, b = entry(1 + side, 0, s) - base, entry(1 + side, 1, s) - base
+            live = (s < entry(1 + side, 2, 0)) & (b >= 0) & (b < 8)
             n = append(n, live, (2 + side) * SLOTS + s, place(a), b)
         return n
 
     total = lax.fori_loop(0, SLOTS, listing, 0)
-    for u in range(UNROLL):
+    for u in range(UNROLL + 1):
         t_list[total + u] = 0
         d_list[total + u] = 0
         o_list[total + u] = ATOMS_DEV
 
-    acc[...] = jnp.zeros_like(acc)
+    def build(at, u):
+        t = t_list[at]
+        group, s = lax.shift_right_logical(t, 4), t & 15
+        for m in range(MODES):
+            right = right_cc[group, m, pl.ds(s, PADROW, stride=SLOTS), :]
+            for i in range(NORB):
+                left = left_cc[group, m, pl.ds(i * SLOTS + s, 1), :]
+                kron[u, i * PADROW : (i + 1) * PADROW, m * 128 : (m + 1) * 128] = (left * right).astype(BF16)
 
     def visit(step, carry):
         for u in range(UNROLL):
             at = step * UNROLL + u
-            t, d, o = t_list[at], d_list[at], o_list[at]
-            group, s = lax.shift_right_logical(t, 4), t & 15
-            for m in range(MODES):
-                right = right_cc[group, m, pl.ds(s, PADROW, stride=SLOTS), :]
-                for i in range(NORB):
-                    left = left_cc[group, m, pl.ds(i * SLOTS + s, 1), :]
-                    kron[u, i * PADROW : (i + 1) * PADROW, m * 128 : (m + 1) * 128] = (left * right).astype(BF16)
-            acc[o] += jnp.dot(kron[u], data[d], preferred_element_type=F32)
+            d, o = d_list[at], o_list[at]
+            term = jnp.dot(kron[u], data[d], preferred_element_type=F32)
+            build(at + 1, (u + 1) % UNROLL)
+            acc[o] += term
         return carry
 
+    build(0, 0)
     lax.fori_loop(0, lax.div(total + UNROLL - 1, UNROLL), visit, 0)
 
     for o in range(ATOMS_DEV):
@@ -324,34 +353,39 @@
         out[o] = jnp.dot(collect[...], tall, preferred_element_type=F32).astype(BF16)
 
 
-def born(meta, mn, *arrays):
+def born(*arrays):
     vm = pl.BlockSpec(memory_space=pltpu.VMEM)
-    sm = pl.BlockSpec(memory_space=pltpu.SMEM)
     return pl.pallas_call(
         born_kernel,
         out_shape=jax.ShapeDtypeStruct((ATOMS_DEV, 2 * SQ, E_DEV), BF16),
-        in_specs=[sm] * 2 + [vm] * len(arrays),
+        in_specs=[vm] * len(arrays),
         out_specs=vm,
         scratch_shapes=[
             pltpu.VMEM((ATOMS_DEV + 1, KR, 2 * E_DEV), F32),
             pltpu.VMEM((UNROLL, KR, MODES * 128), BF16),
-            pltpu.SMEM((4 * SLOTS + UNROLL,), jnp.int32),
-            pltpu.SMEM((4 * SLOTS + UNROLL,), jnp.int32),
-            pltpu.SMEM((4 * SLOTS + UNROLL,), jnp.int32),
+            pltpu.VMEM((2 * SQ, 2 * KR), BF16),
+            pltpu.SMEM((3, 8, 128), F32),
+            pltpu.SMEM((4 * SLOTS + UNROLL + 1,), jnp.int32),
+            pltpu.SMEM((4 * SLOTS + UNROLL + 1,), jnp.int32),
+            pltpu.SMEM((4 * SLOTS + UNROLL + 1,), jnp.int32),
+            pltpu.SemaphoreType.DMA((3,)),
         ],
         compiler_params=pltpu.CompilerParams(vmem_limit_bytes=32 * 2**20),
         name="born",
-    )(meta, mn, *arrays)
+    )(*arrays)
 
 
 def per_device(na, ne, green, coupling, pairs, counts, occupation, offsets):
-    meta = jnp.concatenate([pairs.T, jnp.broadcast_to(counts, (1, SLOTS))], axis=0)
-    spread, collect = row_tables()
-    tables = jnp.asarray(expansion_tables(), BF16)
-    data, left_cc, right_cc, mn = exchange(
-        na, ne, occupation, offsets, green, coupling, meta, tables, jnp.asarray(spread, BF16)
+    def row(x):
+        x = x.astype(F32).reshape(-1, x.shape[-1])
+        return jnp.pad(x, ((0, 0), (0, coupling.shape[1] - x.shape[1])))
+
+    pack = jnp.concatenate(
+        [coupling.astype(F32), row(pairs.T), row(counts), row(occupation), row(offsets), jnp.zeros((3, coupling.shape[1]), F32)],
+        axis=0,
     )
-    return born(meta, mn, data, left_cc, right_cc, jnp.asarray(collect, BF16))
+    data, left_cc, right_cc, pack_n = exchange(na, ne, green, pack)
+    return born(pack, pack_n, data, left_cc, right_cc)
 
 
 def solution(mesh):

time: 34.2 us -> 30.4 us (0.89)
  the two profiles are of different devices: /device:TPU:1 before, /device:TPU:19 now
where the time goes in v2:
time: 30.4 us
  Pallas kernels  25.9 us (85%)
  local copies, waits for them, and re-layouts  2.47 us (8%)
  other arithmetic  1.34 us (4%)
  between operations  0.69 us (2%)
    pallas_call x1, Pallas kernels, exchange(): pl.pallas_call(functools.partial(exchange_kernel, na, ne), out_shape=[sha...  15.6 us
    pallas_call x1, Pallas kernels, born(): pl.pallas_call(born_kernel, out_shape=jax.ShapeDtypeStruct((ATOMS_DEV, 2...  10.3 us
    unnamed x2, local copies, waits for them, and re-layouts  1 us
    concatenate x1, local copies, waits for them, and re-layouts, per_device(): jnp.concatenate([coupling.astype(F32), row(pairs.T), row(counts), row(occ...  0.8 us
    convert_element_type x1, other arithmetic, row(): x = x.astype(F32).reshape(-1, x.shape[-1])  0.68 us
    pad x4, local copies, waits for them, and re-layouts, row(): return jnp.pad(x, ((0, 0), (0, coupling.shape[1] - x.shape[1])))  0.68 us
    reshape x1, other arithmetic, row(): x = x.astype(F32).reshape(-1, x.shape[-1])  0.66 us

profile of v2, /device:TPU:19, one launch (start us, length us, event | category | flops | bytes accessed | tf_op | source)
XLA Modules:
  0.0 30.4 jit_solution(8462968849524592780)
XLA Ops:
  0.7 0.7 %convert_bitcast_fusion.1 = f32[1,8]{1,0:T(1,128)S(1)} fusion(s32[8]{0:T(128)} %param.11), kind=kLoop, calls=%fused_computation.1 | loop fusion | flops 8 | bytes 64 | tf_op jit(solution)/shard_map/reshape | solution.py:380
  1.3 0.7 %convert_bitcast_fusion = f32[2,16]{1,0:T(2,128)S(1)} fusion(s32[16,2]{0,1:T(2,128)} %param.8), kind=kLoop, calls=%fused_computation | loop fusion | flops 32 | bytes 256 | tf_op jit(solution)/shard_map/convert_element_type | solution.py:380
  2.0 0.7 %pad.17 = f32[1,800]{1,0:T(1,128)S(1)} pad(f32[1,8]{1,0:T(1,128)} %bitcast.6, f32[]{:T(128)} %constant.1.clone.1), padding=0_0x0_792 | pad | bytes 3236 | tf_op jit(solution)/shard_map/jit(_pad)/pad | solution.py:381
  2.7 0.8 %concatenate.3.pack = f32[24,800]{1,0:T(8,128)S(1)} concatenate(bf16[16,800]{1,0:T(8,128)(2,1)} %param.7, f32[2,800]{1,0:T(2,128)S(1)} %pad.15, f32[1,800]{1,0:T(1,128)S(1)} %pad.16, f32[1,800]{1,0:T(1,128)S(1)} %pad.17, f32[1,800]{1,0:T(1,128)S(1)} %pad.18, f32[3,800]{1,0:T(4,128)S(1)} %broadcast_in_dim.3), dimensions={0} | concatenate | bytes 128000 | tf_op jit(solution)/shard_map/concatenate | solution.py:383
  3.5 0.0 copy-start
  3.5 1.0 %copy-done = bf16[8,200,128]{2,1,0:T(8,128)(2,1)S(1)} copy-done((bf16[8,200,128]{2,1,0:T(8,128)(2,1)S(1)}, bf16[8,200,128]{2,1,0:T(8,128)(2,1)}, u32[]{:S(2)}) %copy-start) | copy-done | bytes 409624
  4.5 15.6 %exchange.1 = (bf16[12,1024,256]{2,1,0:T(8,128)(2,1)S(1)}, f32[4,8,256,128]{3,2,1,0:T(8,128)S(1)}, f32[4,8,256,128]{3,2,1,0:T(8,128)S(1)}, f32[2,24,800]{2,1,0:T(8,128)S(1)}) custom-call(bf16[8,200,128]{2,1,0:T(8,128)(2,1)S(1)} %copy-done, f32[24,800]{1,0:T(8,128)S(1)} %concatenate.3.pack), custom_call_target="tpu_custom_call" | custom-call | tf_op jit(solution)/shard_map/exchange/pallas_call | solution.py:252
  20.1 10.3 %born.1 = bf16[8,200,128]{2,1,0:T(8,128)(2,1)} custom-call(f32[24,800]{1,0:T(8,128)S(1)} %concatenate.3.pack, f32[2,24,800]{2,1,0:T(8,128)S(1)} %get-tuple-element.9.pack_n, bf16[12,1024,256]{2,1,0:T(8,128)(2,1)S(1)} %get-tuple-element.10.data, f32[4,8,256,128]{3,2,1,0:T(8,128)S(1)} %get-tuple-element.11.left_cc, ...), custom_call_target="tpu_custom_call" | custom-call | tf_op jit(solution)/shard_map/born/pallas_call | solution.py:358
  (4 shorter events, 0.0 us)
Async XLA Ops:
  3.5 1.0 %copy-start = (bf16[8,200,128]{2,1,0:T(8,128)(2,1)S(1)}, bf16[8,200,128]{2,1,0:T(8,128)(2,1)}, u32[]{:S(2)}) copy-start(bf16[8,200,128]{2,1,0:T(8,128)(2,1)} %green.1) | copy-start | bytes 1228804
